TPU v7x, 32 devices: a whole 2x2x4 slice. The times are simulated.
32 devices in a mesh: batch: 2 (over y), region: 4 (over z), scen: 2 (over x), row: 2 (over core).
Axes of the slice: x: 2, y: 2, z: 4, core: 2. Of those that a mesh axis runs over, the one named last changes fastest.
Arguments:
- kkt_inverse: bfloat16 [4, 1536, 1536], P('region', 'row'), may hold values from -0.25 to 1.25, as said below
- bus_load: bfloat16 [4, 1536, 1024], P('region', None, ('batch', 'scen', 'row')), parts along dimension 2, may hold values from -6 to 6
- bus_limit: float32 [4, 1536], P('region'), may hold values from 0.3 to 3
- copy_local: int32 [4, 128], P('region'), may hold values from 0 to 1535, as said below
- copy_dest: int32 [4, 128], P('region'), may hold values from 0 to 3, as said below
- copy_slot: int32 [4, 128], P('region'), may hold values from 0 to 63, as said below
- copy_key: int32 [4, 128], P('region'), may hold values from 0 to 63
- own_key: int32 [4, 4, 64], P('region'), may hold values from -1 to 63, as said below
Outputs:
- dispatch: float32 [4, 1536, 1024], P('region', None, ('batch', 'scen', 'row')), parts along dimension 2
- scaled_duals: float32 [4, 128, 1024], P('region', None, ('batch', 'scen', 'row')), parts along dimension 2
There are 2 independent parts, one for each index of `batch`. A program takes and returns all parts, laid end to end along the dimension named above; an argument that names none is the same for every part. Nothing has to cross between parts.
Inputs may be any that keep to these rules, and one draw needn't show every extreme that they name: `copy_local`: the 128 local buses of one region's copies are distinct. `copy_dest`: A region sends at most 64 copies to one owner; in every draw one owner receives exactly 64 copies from every region. `copy_slot`: within one region, copies with the same owner have distinct slots. own_key[o, r, s] equals copy_key[r, k] for the copy k of region r with copy_dest o and copy_slot s, and -1 where region r has no such copy. `kkt_inverse`: each matrix has a diagonal of 0.75 to 1.25 and independent off-diagonal entries.
All inputs are finite; a program needn't handle non-finite values.
Results may differ from a plain program's by a relative error of at most 0.0026.
Values may be sent and summed in bfloat16 or wider, within the bound.
A program may use at most 64 MiB of HBM per device.

v0:
```python
import jax
import jax.numpy as jnp
from jax import lax
from jax.sharding import PartitionSpec as P

GO = 64
ITERS = 3


PENALTY = 1.0
PROXIMAL = 0.5


def per_device(
    kkt_inverse, bus_load, bus_limit, copy_local, copy_dest, copy_slot, copy_key, own_key
):
    inverse_rows = kkt_inverse[0]
    load_cols = bus_load[0].astype(jnp.float32)
    limit_all = bus_limit[0]
    local_rows = copy_local[0]
    dest_rows = copy_dest[0]
    slot_rows = copy_slot[0]
    owner_keys = own_key[0].reshape(-1)
    regions = lax.axis_size("region")
    capacity = own_key.shape[2]
    bus_count = load_cols.shape[0]
    column_count = load_cols.shape[1]
    copy_count = local_rows.shape[0]
    send_rows = dest_rows * capacity + slot_rows
    selector = (owner_keys[None, :] == jnp.arange(GO, dtype=jnp.int32)[:, None]).astype(jnp.float32)
    tallies = jnp.maximum(jnp.sum(selector, axis=1), 1.0)
    fetch_rows = jnp.where(owner_keys >= 0, owner_keys, 0)
    dispatch = jnp.zeros((bus_count, column_count), jnp.float32)
    dual_vals = jnp.zeros((copy_count, column_count), jnp.float32)
    consensus = jnp.zeros((copy_count, column_count), jnp.float32)
    for iteration in range(ITERS):
        boundary = (
            jnp.zeros((bus_count, column_count), jnp.float32)
            .at[local_rows]
            .add(consensus - dual_vals)
        )
        drive_cols = (load_cols + PROXIMAL * dispatch + PENALTY * boundary).astype(jnp.bfloat16)
        half_rows = inverse_rows.shape[0]
        first_row = lax.axis_index("row") * half_rows
        limit_half = lax.dynamic_slice_in_dim(limit_all, first_row, half_rows, 0)
        solved = jnp.dot(
            inverse_rows,
            lax.all_gather(drive_cols, "row", axis=1, tiled=True),
            preferred_element_type=jnp.float32,
        )
        clipped = jnp.clip(solved, -limit_half[:, None], limit_half[:, None])
        dispatch = lax.all_to_all(clipped, "row", split_axis=1, concat_axis=0, tiled=True)
        at_copies = dispatch[local_rows]
        shared = at_copies + dual_vals
        packed = (
            jnp.zeros((regions * capacity, column_count), jnp.float32).at[send_rows].set(shared)
        )
        packed = packed.reshape(regions, capacity, column_count)
        arrived = lax.all_to_all(packed, "region", split_axis=0, concat_axis=0, tiled=True)
        totals = jnp.dot(
            selector,
            arrived.reshape(-1, column_count),
            precision=lax.Precision.HIGHEST,
            preferred_element_type=jnp.float32,
        )
        averages = totals / tallies[:, None]
        replies = averages[fetch_rows].reshape(regions, capacity, column_count)
        answered = lax.all_to_all(replies, "region", split_axis=0, concat_axis=0, tiled=True)
        consensus = answered.reshape(-1, column_count)[send_rows]
        dual_vals = dual_vals + at_copies - consensus
    return (dispatch[None], dual_vals[None])


def solution(mesh):
    return jax.shard_map(
        per_device,
        mesh=mesh,
        in_specs=(
            P("region", "row", None),
            P("region", None, ("batch", "scen", "row")),
            P("region", None),
            P("region", None),
            P("region", None),
            P("region", None),
            P("region", None),
            P("region", None, None),
        ),
        out_specs=(
            P("region", None, ("batch", "scen", "row")),
            P("region", None, ("batch", "scen", "row")),
        ),
        check_vma=False,
    )
```

profile of v0, /device:TPU:0, one launch (start us, length us, event | category | flops | bytes accessed | tf_op | source)
XLA Modules:
  0.0 114.2 jit_solution(6413281735627667836)
XLA Ops:
  3.2 1.6 %scatter_custom_fusion = f32[1536,128]{1,0:T(8,128)S(1)} fusion(f32[1536,128]{1,0:T(8,128)S(1)} %bitcast_convert_fusion, s32[128]{0:T(128)S(1)} %fusion.39, f32[]{:T(128)} %constant.13.clone.1), kind=kCustom, calls=%fused_computation.46 | custom fusion | flops 16384 | bytes 786436 | tf_op jit(solution)/shard_map/scatter-add | solution.py:40
  4.8 2.4 %all_gather.9 = bf16[1536,256]{1,0:T(8,128)(2,1)S(1)} all-gather(bf16[1536,128]{1,0:T(8,128)(2,1)S(1)} %convert_element_type.20), channel_id=1, replica_groups=mesh['batch'=2,'region'=4,'scen'=2,'row'=2] {'row'}, dimensions={1}, use_global_device_ids=true | all-gather | bytes 1179648 | tf_op jit(solution)/shard_map/all_gather | solution.py:48
  7.3 1.7 %fusion.9 = f32[256,768]{1,0:T(8,128)} fusion(bf16[1536,256]{1,0:T(8,128)(2,1)S(1)} %all_gather.9, bf16[1,768,1536]{2,1,0:T(8,128)(2,1)S(1)} %copy-done, f32[768]{0:T(1024)S(1)} %neg.10, f32[768]{0:T(1024)S(1)} %dynamic-slice_reduce_fusion), kind=kOutput, calls=%fused_computation.22 | convolution fusion | flops 604372992 | bytes 3938304 | tf_op jit(solution)/shard_map/dot_general | solution.py:46
  9.0 3.7 %all-to-all-start = ((f32[768,2,128]{0,2,1:T(8,128)}), f32[768,2,128]{0,2,1:T(8,128)S(1)}, u32[]{:S(2)}, u32[]{:S(2)}) async-start(f32[768,2,128]{0,2,1:T(8,128)} %bitcast.84), calls=%async_computation | async-start | bytes 1572864 | tf_op jit(solution)/shard_map/all_to_all | solution.py:52
  12.7 1.9 %all-to-all-done = f32[768,2,128]{0,2,1:T(8,128)S(1)} async-done(((f32[768,2,128]{0,2,1:T(8,128)}), f32[768,2,128]{0,2,1:T(8,128)S(1)}, u32[]{:S(2)}, u32[]{:S(2)}) %all-to-all-start) | async-done | bytes 786464 | tf_op jit(solution)/shard_map/all_to_all | solution.py:52
  17.5 1.5 %scatter_custom_fusion.1 = f32[256,128]{1,0:T(8,128)} fusion(s32[128]{0:T(128)S(1)} %fusion.40, f32[128,128]{1,0:T(8,128)S(1)} %gather_fusion, f32[]{:T(128)} %constant.13.clone.1), kind=kCustom, calls=%fused_computation.43 | custom fusion | bytes 131076 | tf_op jit(solution)/shard_map/scatter | solution.py:56
  19.0 6.2 %all-to-all-start.1 = ((f32[4,64,128]{2,1,0:T(8,128)}), f32[4,64,128]{2,1,0:T(8,128)S(1)}, u32[]{:S(2)}, u32[]{:S(2)}) async-start(f32[4,64,128]{2,1,0:T(8,128)} %bitcast.11), calls=%async_computation.1 | async-start | bytes 262144 | tf_op jit(solution)/shard_map/all_to_all | solution.py:59
  25.6 5.9 %all-to-all-done.1 = f32[4,64,128]{2,1,0:T(8,128)S(1)} async-done(((f32[4,64,128]{2,1,0:T(8,128)}), f32[4,64,128]{2,1,0:T(8,128)S(1)}, u32[]{:S(2)}, u32[]{:S(2)}) %all-to-all-start.1) | async-done | bytes 131104 | tf_op jit(solution)/shard_map/all_to_all | solution.py:59
  33.0 3.3 %all-to-all-start.2 = ((f32[4,64,128]{2,1,0:T(8,128)}), f32[4,64,128]{2,1,0:T(8,128)S(1)}, u32[]{:S(2)}, u32[]{:S(2)}) async-start(f32[4,64,128]{2,1,0:T(8,128)} %bitcast.14), calls=%async_computation.2 | async-start | bytes 262144 | tf_op jit(solution)/shard_map/all_to_all | solution.py:68
  36.3 2.0 %multiply_add_fusion.1 = f32[1536,128]{1,0:T(8,128)} fusion(bf16[1,1536,128]{2,1,0:T(8,128)(2,1)} %param.9, f32[2,768,128]{2,1,0:T(8,128)S(1)} %copy.13), kind=kLoop, calls=%fused_computation.31 | loop fusion | flops 589824 | bytes 1966080 | tf_op jit(solution)/shard_map/add | solution.py:42
  38.3 3.9 %all-to-all-done.2 = f32[4,64,128]{2,1,0:T(8,128)S(1)} async-done(((f32[4,64,128]{2,1,0:T(8,128)}), f32[4,64,128]{2,1,0:T(8,128)S(1)}, u32[]{:S(2)}, u32[]{:S(2)}) %all-to-all-start.2) | async-done | bytes 131104 | tf_op jit(solution)/shard_map/all_to_all | solution.py:68
  42.9 3.2 %scatter_custom_fusion.2 = f32[1536,128]{1,0:T(8,128)} fusion(f32[1536,128]{1,0:T(8,128)} %multiply_add_fusion.1, s32[128]{0:T(128)S(1)} %fusion.39, f32[128,128]{1,0:T(8,128)S(1)} %gather_fusion.2, f32[128,128]{1,0:T(8,128)S(1)} %sub.42), kind=kCustom, calls=%fused_computation.36 | custom fusion | flops 32768 | bytes 917504 | tf_op jit(solution)/shard_map/scatter-add | solution.py:40
  47.2 2.4 %all_gather.10 = bf16[1536,256]{1,0:T(8,128)(2,1)S(1)} all-gather(bf16[1536,128]{1,0:T(8,128)(2,1)S(1)} %convert_element_type.22), channel_id=1, replica_groups=mesh['batch'=2,'region'=4,'scen'=2,'row'=2] {'row'}, dimensions={1}, use_global_device_ids=true | all-gather | bytes 1179648 | tf_op jit(solution)/shard_map/all_gather | solution.py:48
  50.4 5.1 %all_to_all.87 = f32[768,2,128]{0,2,1:T(8,128)} all-to-all(f32[768,2,128]{0,2,1:T(8,128)S(1)} %bitcast.86), channel_id=1, replica_groups=mesh['batch'=2,'region'=4,'scen'=2,'row'=2] {'row'}, dimensions={1} | all-to-all | bytes 1572864 | tf_op jit(solution)/shard_map/all_to_all | solution.py:52
  58.5 8.9 %all_to_all.88 = f32[4,64,128]{2,1,0:T(8,128)S(1)} all-to-all(f32[4,64,128]{2,1,0:T(8,128)S(1)} %bitcast.91), channel_id=1, replica_groups=mesh['batch'=2,'region'=4,'scen'=2,'row'=2] {'region'}, dimensions={0} | all-to-all | bytes 262144 | tf_op jit(solution)/shard_map/all_to_all | solution.py:59
  68.9 3.3 %all-to-all-start.5 = ((f32[4,64,128]{2,1,0:T(8,128)}), f32[4,64,128]{2,1,0:T(8,128)S(1)}, u32[]{:S(2)}, u32[]{:S(2)}) async-start(f32[4,64,128]{2,1,0:T(8,128)} %bitcast.22), calls=%async_computation.5 | async-start | bytes 262144 | tf_op jit(solution)/shard_map/all_to_all | solution.py:68
  72.2 2.0 %multiply_add_fusion = f32[1536,128]{1,0:T(8,128)} fusion(bf16[1,1536,128]{2,1,0:T(8,128)(2,1)} %param.9, f32[2,768,128]{2,1,0:T(8,128)S(1)} %copy.14), kind=kLoop, calls=%fused_computation.30 | loop fusion | flops 589824 | bytes 1966080 | tf_op jit(solution)/shard_map/add | solution.py:42
  74.2 3.9 %all-to-all-done.5 = f32[4,64,128]{2,1,0:T(8,128)S(1)} async-done(((f32[4,64,128]{2,1,0:T(8,128)}), f32[4,64,128]{2,1,0:T(8,128)S(1)}, u32[]{:S(2)}, u32[]{:S(2)}) %all-to-all-start.5) | async-done | bytes 131104 | tf_op jit(solution)/shard_map/all_to_all | solution.py:68
  78.8 3.2 %scatter_custom_fusion.4 = f32[1536,128]{1,0:T(8,128)} fusion(f32[1536,128]{1,0:T(8,128)} %multiply_add_fusion, s32[128]{0:T(128)S(1)} %fusion.39, f32[128,128]{1,0:T(8,128)S(1)} %gather_fusion.5, f32[128,128]{1,0:T(8,128)S(1)} %sub.44), kind=kCustom, calls=%fused_computation.34 | custom fusion | flops 32768 | bytes 917504 | tf_op jit(solution)/shard_map/scatter-add | solution.py:40
  83.1 2.4 %all_gather.11 = bf16[1536,256]{1,0:T(8,128)(2,1)S(1)} all-gather(bf16[1536,128]{1,0:T(8,128)(2,1)S(1)} %convert_element_type.23), channel_id=1, replica_groups=mesh['batch'=2,'region'=4,'scen'=2,'row'=2] {'row'}, dimensions={1}, use_global_device_ids=true | all-gather | bytes 1179648 | tf_op jit(solution)/shard_map/all_gather | solution.py:48
  86.3 4.4 %all_to_all.89 = f32[768,2,128]{0,2,1:T(8,128)S(1)} all-to-all(f32[768,2,128]{0,2,1:T(8,128)S(1)} %bitcast.85), channel_id=1, replica_groups=mesh['batch'=2,'region'=4,'scen'=2,'row'=2] {'row'}, dimensions={1} | all-to-all | bytes 1572864 | tf_op jit(solution)/shard_map/all_to_all | solution.py:52
  91.9 1.8 %gather_fusion.6 = f32[128,128]{1,0:T(8,128)S(1)} fusion(f32[1536,128]{1,0:T(8,128)} %bitcast.82, s32[1024]{0:T(1024)S(1)} %pad_clamp_fusion.2), kind=kCustom, calls=%fused_computation.6 | custom fusion | bytes 131584 | tf_op jit(solution)/shard_map/gather | solution.py:53
  94.6 8.9 %all_to_all.90 = f32[4,64,128]{2,1,0:T(8,128)S(1)} all-to-all(f32[4,64,128]{2,1,0:T(8,128)S(1)} %bitcast.90), channel_id=1, replica_groups=mesh['batch'=2,'region'=4,'scen'=2,'row'=2] {'region'}, dimensions={0} | all-to-all | bytes 262144 | tf_op jit(solution)/shard_map/all_to_all | solution.py:59
  104.4 8.6 %all_to_all.91 = f32[4,64,128]{2,1,0:T(8,128)S(1)} all-to-all(f32[4,64,128]{2,1,0:T(8,128)S(1)} %bitcast.92), channel_id=1, replica_groups=mesh['batch'=2,'region'=4,'scen'=2,'row'=2] {'region'}, dimensions={0} | all-to-all | bytes 262144 | tf_op jit(solution)/shard_map/all_to_all | solution.py:68
  (49 shorter events, 21.4 us)
Async XLA Ops:
  0.6 6.7 %copy-start = (bf16[1,768,1536]{2,1,0:T(8,128)(2,1)S(1)}, bf16[1,768,1536]{2,1,0:T(8,128)(2,1)}, u32[]{:S(2)}) copy-start(bf16[1,768,1536]{2,1,0:T(8,128)(2,1)} %param.8) | copy-start | bytes 7077892
  9.0 7.9 %copy-start.3 = (s32[1,128]{1,0:T(1,128)S(1)}, s32[1,128]{1,0:T(1,128)}, u32[]{:S(2)}) copy-start(s32[1,128]{1,0:T(1,128)} %param.13) | copy-start | bytes 1540
  9.0 7.9 %copy-start.4 = (s32[1,128]{1,0:T(1,128)S(1)}, s32[1,128]{1,0:T(1,128)}, u32[]{:S(2)}) copy-start(s32[1,128]{1,0:T(1,128)} %param.12) | copy-start | bytes 1540
  9.0 16.3 %copy-start.2 = (s32[1,4,64]{2,1,0:T(4,128)S(1)}, s32[1,4,64]{2,1,0:T(4,128)}, u32[]{:S(2)}) copy-start(s32[1,4,64]{2,1,0:T(4,128)} %param.14) | copy-start | bytes 3076
  9.0 5.6 %all-to-all-start = ((f32[768,2,128]{0,2,1:T(8,128)}), f32[768,2,128]{0,2,1:T(8,128)S(1)}, u32[]{:S(2)}, u32[]{:S(2)}) async-start(f32[768,2,128]{0,2,1:T(8,128)} %bitcast.84), calls=%async_computation | async-start | bytes 1572864 | tf_op jit(solution)/shard_map/all_to_all | solution.py:52
  14.6 0.9 copy-start.1
  19.0 12.5 %all-to-all-start.1 = ((f32[4,64,128]{2,1,0:T(8,128)}), f32[4,64,128]{2,1,0:T(8,128)S(1)}, u32[]{:S(2)}, u32[]{:S(2)}) async-start(f32[4,64,128]{2,1,0:T(8,128)} %bitcast.11), calls=%async_computation.1 | async-start | bytes 262144 | tf_op jit(solution)/shard_map/all_to_all | solution.py:59
  33.0 9.2 %all-to-all-start.2 = ((f32[4,64,128]{2,1,0:T(8,128)}), f32[4,64,128]{2,1,0:T(8,128)S(1)}, u32[]{:S(2)}, u32[]{:S(2)}) async-start(f32[4,64,128]{2,1,0:T(8,128)} %bitcast.14), calls=%async_computation.2 | async-start | bytes 262144 | tf_op jit(solution)/shard_map/all_to_all | solution.py:68
  68.9 9.2 %all-to-all-start.5 = ((f32[4,64,128]{2,1,0:T(8,128)}), f32[4,64,128]{2,1,0:T(8,128)S(1)}, u32[]{:S(2)}, u32[]{:S(2)}) async-start(f32[4,64,128]{2,1,0:T(8,128)} %bitcast.22), calls=%async_computation.5 | async-start | bytes 262144 | tf_op jit(solution)/shard_map/all_to_all | solution.py:68
where the time goes:
time: 115 us; the launch traced here: 114 us
  blocking collectives  43 us (37%)
  local copies, waits for them, and re-layouts  17.4 us (15%)
  other arithmetic  16.9 us (15%)
  starting transfers between devices  16.6 us (14%)
  waiting for transfers between devices  15.7 us (14%)
  matrix products  3.9 us (3%)
    all_to_all x2, blocking collectives, per_device(): lax.all_to_all(packed, 'region', split_axis=0, concat_axis=0, tiled=True)  17.8 us
    all_to_all x2, blocking collectives, per_device(): lax.all_to_all(clipped, 'row', split_axis=1, concat_axis=0, tiled=True)  9.49 us
    all_to_all x1, blocking collectives, per_device(): lax.all_to_all(replies, 'region', split_axis=0, concat_axis=0, tiled=True)  8.59 us
    scatter-add x3, other arithmetic, per_device(): boundary = jnp.zeros((bus_count, column_count), jnp.float32).at[local_row...  7.89 us
    all_to_all x2, waiting for transfers between devices, per_device(): lax.all_to_all(replies, 'region', split_axis=0, concat_axis=0, tiled=True)  7.86 us
    all_gather x3, blocking collectives, per_device(): lax.all_gather(drive_cols, 'row', axis=1, tiled=True)  7.19 us
    all_to_all x2, starting transfers between devices, per_device(): lax.all_to_all(replies, 'region', split_axis=0, concat_axis=0, tiled=True)  6.65 us
    all_to_all x1, starting transfers between devices, per_device(): lax.all_to_all(packed, 'region', split_axis=0, concat_axis=0, tiled=True)  6.24 us
  transfers between devices with their start and end apart: 4, of which 4 were waited for; matrix products, arithmetic and copies ran while one was open for 4% of the time, Pallas kernels for 0%

commit v1 on v0

v1 whole, which is shorter than its diff:
```python
import functools

import jax
import jax.numpy as jnp
from jax import lax
from jax.experimental import pallas as pl
from jax.experimental.pallas import tpu as pltpu
from jax.sharding import PartitionSpec as P

ITERS = 3
PENALTY = 1.0
PROXIMAL = 0.5

MESH = pl.DeviceIdType.MESH
F32 = jnp.float32
BF16 = jnp.bfloat16


def wide(a, b):
    return jnp.dot(a, b, preferred_element_type=F32)


def halves(x):
    hi = x.astype(BF16)
    lo = (x - hi.astype(F32)).astype(BF16)
    return hi, lo


def kernel(
    regions, rows, step, link,
    inv_ref, load_ref, limit_ref, local_ref, dest_ref, key_ref,
    disp_ref, dual_ref,
    full, first_rhs, part, limits, load_in, prox_in, columns, drive, pick, gathered,
    outbox, inbox, id_out, id_in,
    own_sem, full_send, full_recv, id_send, id_recv, box_send, box_recv,
):
    me = lax.axis_index("region")
    row = lax.axis_index("row")
    half = inv_ref.shape[1]
    buses, cols = load_ref.shape[1], load_ref.shape[2]
    copies = local_ref.shape[1]
    chunks = half // step
    first_row = row * half
    peers = [lax.rem(me + j, regions) for j in range(1, regions)]
    mates = [lax.rem(row + j, rows) for j in range(1, rows)]

    barrier = pltpu.get_barrier_semaphore()
    for mate in mates:
        pl.semaphore_signal(barrier, inc=1, device_id={"row": mate}, device_id_type=MESH)
    for peer in peers:
        pl.semaphore_signal(barrier, inc=1, device_id={"region": peer}, device_id_type=MESH)

    own_copies = []
    for c in range(chunks):
        copy = pltpu.make_async_copy(
            inv_ref.at[0, pl.ds(c * step, step)],
            full.at[pl.ds(pl.multiple_of(first_row + c * step, step), step)],
            own_sem.at[c],
        )
        copy.start()
        own_copies.append(copy)
    ids = (key_ref[...] * regions + dest_ref[...]).astype(F32)
    id_out[...] = jnp.broadcast_to(ids, id_out.shape)

    pl.semaphore_wait(barrier, len(mates) + len(peers))
    full_copies = []
    for c in range(chunks):
        for j, mate in enumerate(mates):
            copy = pltpu.make_async_remote_copy(
                src_ref=inv_ref.at[0, pl.ds(c * step, step)],
                dst_ref=full.at[pl.ds(pl.multiple_of(first_row + c * step, step), step)],
                send_sem=full_send.at[j, c],
                recv_sem=full_recv.at[j, c],
                device_id={"row": mate},
                device_id_type=MESH,
            )
            copy.start()
            full_copies.append((c, j, copy))
    id_copies = []
    for j, peer in enumerate(peers):
        copy = pltpu.make_async_remote_copy(
            src_ref=id_out,
            dst_ref=id_in.at[j],
            send_sem=id_send.at[j],
            recv_sem=id_recv.at[j],
            device_id={"region": peer},
            device_id_type=MESH,
        )
        copy.start()
        id_copies.append(copy)

    local_row = local_ref[...].astype(F32)
    local_col = jnp.transpose(jnp.broadcast_to(local_row, (copies, copies)))[:, :1]
    bus_lane = lax.broadcasted_iota(jnp.int32, (copies, buses), 1).astype(F32)
    pick[...] = jnp.where(bus_lane == local_col, 1.0, 0.0).astype(BF16)
    bus_sub = lax.broadcasted_iota(jnp.int32, (buses, copies), 0).astype(F32)
    place = jnp.where(bus_sub == local_row, 1.0, 0.0).astype(BF16)
    first_rhs[:, :cols] = load_ref[0]
    first_rhs[:, cols:] = place
    inner = 1.0 - wide(place, jnp.ones((copies, cols), BF16))
    load_in[...] = (load_ref[0].astype(F32) * inner).astype(BF16)
    prox_in[...] = PROXIMAL * inner
    for block in range(0, buses, cols):
        piece = jnp.broadcast_to(limit_ref[:, block:block + cols], (cols, cols))
        limits[block:block + cols, :] = jnp.transpose(piece)
    load_at = wide(pick[...], load_ref[0])
    top = limits[...].astype(BF16)
    rest = limits[...] - top.astype(F32)
    mid = rest.astype(BF16)
    low = (rest - mid.astype(F32)).astype(BF16)
    limit_at = wide(pick[...], top) + wide(pick[...], mid) + wide(pick[...], low)

    gathered[...] = jnp.zeros_like(gathered)

    def first_chunk(at):
        at = pl.multiple_of(at, step)
        rows_at = pl.ds(at, step)
        prod = wide(full[rows_at, :], first_rhs[...])
        picked = prod[:, cols:].astype(BF16)
        columns[rows_at, :] = picked
        bound = limits[rows_at, :]
        value = jnp.clip(prod[:, :cols], -bound, bound)
        disp_ref[0, rows_at, :] = value
        hi, lo = halves(value)
        gathered[...] += wide(pick[:, rows_at], jnp.concatenate([hi, lo, picked], axis=1))

    for c in range(chunks):
        own_copies[c].wait()
        first_chunk(first_row + c * step)
    for c, j, copy in full_copies:
        copy.wait()
        first_chunk(lax.rem(row + rows - j - 1, rows) * half + c * step)
    at_copies = gathered[:, :cols] + gathered[:, cols:2 * cols]
    columns_at = gathered[:, 2 * cols:].astype(BF16)
    duals = jnp.zeros((copies, cols), F32)

    matches = None
    for it in range(ITERS):
        shared = at_copies + duals
        outbox[it] = shared.astype(link)
        box_copies = []
        for j, peer in enumerate(peers):
            copy = pltpu.make_async_remote_copy(
                src_ref=outbox.at[it],
                dst_ref=inbox.at[it, j],
                send_sem=box_send.at[it, j],
                recv_sem=box_recv.at[it, j],
                device_id={"region": peer},
                device_id_type=MESH,
            )
            copy.start()
            box_copies.append(copy)
        if it > 0:
            value = part[...] + wide(columns[...], drive_at)
            disp_ref[0] = jnp.clip(value, -limits[...], limits[...])
        if it < ITERS - 1:
            drive[...] = (load_in[...].astype(F32) + prox_in[...] * disp_ref[0]).astype(BF16)
            gathered[:, :2 * cols] = jnp.zeros((copies, 2 * cols), F32)

            def bulk(i, carry):
                rows_at = pl.ds(pl.multiple_of(i * step, step), step)
                prod = wide(full[rows_at, :], drive[...])
                part[rows_at, :] = prod
                hi, lo = halves(prod)
                gathered[:, :2 * cols] += wide(pick[:, rows_at], jnp.concatenate([hi, lo], axis=1))
                return carry

            lax.fori_loop(0, buses // step, bulk, 0)
        if matches is None:
            id_col = jnp.transpose(jnp.broadcast_to(ids, (copies, copies)))[:, :1]
            for copy in id_copies:
                copy.wait()
            matches = [jnp.where(id_col == ids, 1.0, 0.0).astype(BF16)]
            for j in range(regions - 1):
                matches.append(jnp.where(id_col == id_in[j, :1, :], 1.0, 0.0).astype(BF16))
            tally = functools.reduce(
                lambda a, b: a + b, [wide(m, jnp.ones((copies, cols), BF16)) for m in matches]
            )
            tally = jnp.maximum(tally, 1.0)
        hi, lo = halves(shared)
        total = wide(matches[0], hi) + wide(matches[0], lo)
        for j, copy in enumerate(box_copies):
            copy.wait()
            if link == F32:
                hi, lo = halves(inbox[it, j])
                total += wide(matches[j + 1], hi) + wide(matches[j + 1], lo)
            else:
                total += wide(matches[j + 1], inbox[it, j])
        consensus = total / tally
        duals = duals + at_copies - consensus
        if it < ITERS - 1:
            boundary = consensus - duals
            drive_at = (load_at + PROXIMAL * at_copies + PENALTY * boundary).astype(BF16)
            solved_at = gathered[:, :cols] + gathered[:, cols:2 * cols] + wide(columns_at, drive_at)
            at_copies = jnp.clip(solved_at, -limit_at, limit_at)
    dual_ref[0] = duals


def chunk_rows(half):
    for step in (256, 128):
        if half % step == 0:
            return step
    return half


LINK = F32


def per_device(
    kkt_inverse, bus_load, bus_limit, copy_local, copy_dest, copy_slot, copy_key, own_key
):
    regions = lax.axis_size("region")
    rows = lax.axis_size("row")
    half = kkt_inverse.shape[1]
    buses, cols = bus_load.shape[1], bus_load.shape[2]
    copies = copy_local.shape[1]
    step = chunk_rows(half)
    chunks = half // step
    dma = pltpu.SemaphoreType.DMA
    vmem = pl.BlockSpec(memory_space=pltpu.VMEM)
    return pl.pallas_call(
        functools.partial(kernel, regions, rows, step, LINK),
        out_shape=(
            jax.ShapeDtypeStruct((1, buses, cols), F32),
            jax.ShapeDtypeStruct((1, copies, cols), F32),
        ),
        in_specs=[pl.BlockSpec(memory_space=pl.ANY)] + [vmem] * 5,
        out_specs=(vmem, vmem),
        scratch_shapes=[
            pltpu.VMEM((buses, buses), BF16),
            pltpu.VMEM((buses, cols + copies), BF16),
            pltpu.VMEM((buses, cols), F32),
            pltpu.VMEM((buses, cols), F32),
            pltpu.VMEM((buses, cols), BF16),
            pltpu.VMEM((buses, cols), F32),
            pltpu.VMEM((buses, copies), BF16),
            pltpu.VMEM((buses, cols), BF16),
            pltpu.VMEM((copies, buses), BF16),
            pltpu.VMEM((copies, 2 * cols + copies), F32),
            pltpu.VMEM((ITERS, copies, cols), LINK),
            pltpu.VMEM((ITERS, regions - 1, copies, cols), LINK),
            pltpu.VMEM((8, copies), F32),
            pltpu.VMEM((regions - 1, 8, copies), F32),
            dma((chunks,)),
            dma((rows - 1, chunks)),
            dma((rows - 1, chunks)),
            dma((regions - 1,)),
            dma((regions - 1,)),
            dma((ITERS, regions - 1)),
            dma((ITERS, regions - 1)),
        ],
        compiler_params=pltpu.CompilerParams(
            collective_id=0, has_side_effects=True, vmem_limit_bytes=48 * 1024 * 1024
        ),
    )(kkt_inverse, bus_load, bus_limit, copy_local, copy_dest, copy_key)


def solution(mesh):
    return jax.shard_map(
        per_device,
        mesh=mesh,
        in_specs=(
            P("region", "row", None),
            P("region", None, ("batch", "scen", "row")),
            P("region", None),
            P("region", None),
            P("region", None),
            P("region", None),
            P("region", None),
            P("region", None, None),
        ),
        out_specs=(
            P("region", None, ("batch", "scen", "row")),
            P("region", None, ("batch", "scen", "row")),
        ),
        check_vma=False,
    )
```

time: 115 us -> 39.6 us (0.34)
  blocking collectives: 43 us -> 0 us
  Pallas kernels: 0 us -> 31.8 us
  other arithmetic: 16.9 us -> 0 us
  starting transfers between devices: 16.6 us -> 0 us
  waiting for transfers between devices: 15.7 us -> 0 us
  local copies, waits for them, and re-layouts: 17.4 us -> 6.82 us
  matrix products: 3.9 us -> 0 us
    all_to_all x5 -> x0, blocking collectives: 35.8 us -> none  [the longest x2 17.8 us: per_device(): lax.all_to_all(packed, 'region', split_axis=0, concat_axis=0, tiled=True)]
    pallas_call x0 -> x1, Pallas kernels: none -> 31.8 us  [per_device(): pl.pallas_call(functools.partial(kernel, regions, rows, step, LINK), out_...]
    all_to_all x4 -> x0, starting transfers between devices: 16.6 us -> none  [the longest x2 6.65 us: per_device(): lax.all_to_all(replies, 'region', split_axis=0, concat_axis=0, tiled=True)]
    all_to_all x4 -> x0, waiting for transfers between devices: 15.7 us -> none  [the longest x2 7.86 us: per_device(): lax.all_to_all(replies, 'region', split_axis=0, concat_axis=0, tiled=True)]
    gather x9 -> x0, local copies, waits for them, and re-layouts: 8.39 us -> none  [the longest x3 3.38 us: per_device(): replies = averages[fetch_rows].reshape(regions, capacity, column_count)]
    scatter-add x3 -> x0, other arithmetic: 7.89 us -> none  [per_device(): boundary = jnp.zeros((bus_count, column_count), jnp.float32).at[local_row...]
    all_gather x3 -> x0, blocking collectives: 7.19 us -> none  [per_device(): lax.all_gather(drive_cols, 'row', axis=1, tiled=True)]
    unnamed x10 -> x14, local copies, waits for them, and re-layouts: 0.9 us -> 6.82 us
  transfers between devices with their start and end apart: 4 -> 0, of which waited for: 4 -> 0; matrix products, arithmetic and copies ran while one was open for 4% -> 0% of each run, Pallas kernels for 0% -> 0%
where the time goes in v1:
time: 39.6 us; the launch traced here: 39.3 us
  Pallas kernels  31.8 us (80%)
  local copies, waits for them, and re-layouts  6.82 us (17%)
  between operations  0.65 us (2%)
    pallas_call x1, Pallas kernels, per_device(): pl.pallas_call(functools.partial(kernel, regions, rows, step, LINK), out_...  31.8 us
    unnamed x14, local copies, waits for them, and re-layouts  6.82 us

profile of v1, /device:TPU:0, one launch (start us, length us, event | category | flops | bytes accessed | tf_op | source)
XLA Modules:
  0.0 39.3 jit_solution(9754726560945518668)
XLA Ops:
  0.6 0.0 copy-start
  0.6 1.7 %copy-done = bf16[1,768,1536]{2,1,0:T(8,128)(2,1)S(1)} copy-done((bf16[1,768,1536]{2,1,0:T(8,128)(2,1)S(1)}, bf16[1,768,1536]{2,1,0:T(8,128)(2,1)}, u32[]{:S(2)}) %copy-start) | copy-done | bytes 2359320
  2.3 0.0 copy-start.1
  2.3 1.0 %copy-done.1 = bf16[1,1536,128]{2,1,0:T(8,128)(2,1)S(1)} copy-done((bf16[1,1536,128]{2,1,0:T(8,128)(2,1)S(1)}, bf16[1,1536,128]{2,1,0:T(8,128)(2,1)}, u32[]{:S(2)}) %copy-start.1) | copy-done | bytes 393240
  3.3 0.0 copy-start.2
  3.3 0.7 %copy-done.2 = f32[1,1536]{1,0:T(1,128)S(1)} copy-done((f32[1,1536]{1,0:T(1,128)S(1)}, f32[1,1536]{1,0:T(1,128)}, u32[]{:S(2)}) %copy-start.2) | copy-done | bytes 6168
  4.0 0.0 copy-start.3
  4.0 0.7 %copy-done.3 = s32[1,128]{1,0:T(1,128)S(1)} copy-done((s32[1,128]{1,0:T(1,128)S(1)}, s32[1,128]{1,0:T(1,128)}, u32[]{:S(2)}) %copy-start.3) | copy-done | bytes 536
  4.6 0.0 copy-start.4
  4.6 0.7 %copy-done.4 = s32[1,128]{1,0:T(1,128)S(1)} copy-done((s32[1,128]{1,0:T(1,128)S(1)}, s32[1,128]{1,0:T(1,128)}, u32[]{:S(2)}) %copy-start.4) | copy-done | bytes 536
  5.3 0.0 copy-start.5
  5.3 0.7 %copy-done.5 = s32[1,128]{1,0:T(1,128)S(1)} copy-done((s32[1,128]{1,0:T(1,128)S(1)}, s32[1,128]{1,0:T(1,128)}, u32[]{:S(2)}) %copy-start.5) | copy-done | bytes 536
  6.0 31.8 %shard_map.77 = (f32[1,1536,128]{2,1,0:T(8,128)S(1)}, f32[1,128,128]{2,1,0:T(8,128)S(1)}) custom-call(bf16[1,768,1536]{2,1,0:T(8,128)(2,1)S(1)} %copy-done, bf16[1,1536,128]{2,1,0:T(8,128)(2,1)S(1)} %copy-done.1, f32[1,1536]{1,0:T(1,128)S(1)} %copy-done.2, s32[1,128]{1,0:T(1,128)S(1)} %copy-done.3, s32[1,128]{1,0:T(1,128)S(1)} %copy-done.4, ...), custom_call_target="tpu_custom_call" | custom-call | tf_op jit(solution)/shard_map/pallas_call | solution.py:221
  37.8 0.9 %copy.10 = f32[1,1536,128]{2,1,0:T(8,128)} copy(f32[1,1536,128]{2,1,0:T(8,128)S(1)} %get-tuple-element.4) | data formatting | bytes 1572864
  38.7 0.6 %copy.11 = f32[1,128,128]{2,1,0:T(8,128)} copy(f32[1,128,128]{2,1,0:T(8,128)S(1)} %get-tuple-element.5) | data formatting | bytes 131072
Async XLA Ops:
  0.6 1.7 %copy-start = (bf16[1,768,1536]{2,1,0:T(8,128)(2,1)S(1)}, bf16[1,768,1536]{2,1,0:T(8,128)(2,1)}, u32[]{:S(2)}) copy-start(bf16[1,768,1536]{2,1,0:T(8,128)(2,1)} %inv_ref.1) | copy-start | bytes 7077892
  2.3 1.0 %copy-start.1 = (bf16[1,1536,128]{2,1,0:T(8,128)(2,1)S(1)}, bf16[1,1536,128]{2,1,0:T(8,128)(2,1)}, u32[]{:S(2)}) copy-start(bf16[1,1536,128]{2,1,0:T(8,128)(2,1)} %load_ref.1) | copy-start | bytes 1179652
  3.3 0.7 %copy-start.2 = (f32[1,1536]{1,0:T(1,128)S(1)}, f32[1,1536]{1,0:T(1,128)}, u32[]{:S(2)}) copy-start(f32[1,1536]{1,0:T(1,128)} %limit_ref.1) | copy-start | bytes 18436
  4.0 0.7 %copy-start.3 = (s32[1,128]{1,0:T(1,128)S(1)}, s32[1,128]{1,0:T(1,128)}, u32[]{:S(2)}) copy-start(s32[1,128]{1,0:T(1,128)} %local_ref.1) | copy-start | bytes 1540
  4.6 0.7 %copy-start.4 = (s32[1,128]{1,0:T(1,128)S(1)}, s32[1,128]{1,0:T(1,128)}, u32[]{:S(2)}) copy-start(s32[1,128]{1,0:T(1,128)} %dest_ref.1) | copy-start | bytes 1540
  5.3 0.7 %copy-start.5 = (s32[1,128]{1,0:T(1,128)S(1)}, s32[1,128]{1,0:T(1,128)}, u32[]{:S(2)}) copy-start(s32[1,128]{1,0:T(1,128)} %key_ref.1) | copy-start | bytes 1540

commit v2 on v1

--- a/solution.py
+++ b/solution.py
@@ -28,11 +28,12 @@
 
 def kernel(
     regions, rows, step, link,
-    inv_ref, load_ref, limit_ref, local_ref, dest_ref, key_ref,
+    inv_ref, load_hbm, limit_hbm, local_hbm, dest_hbm, key_hbm,
     disp_ref, dual_ref,
+    load_ref, limit_ref, local_ref, dest_ref, key_ref,
     full, first_rhs, part, limits, load_in, prox_in, columns, drive, pick, gathered,
     outbox, inbox, id_out, id_in,
-    own_sem, full_send, full_recv, id_send, id_recv, box_send, box_recv,
+    in_sem, own_sem, full_send, full_recv, id_send, id_recv, box_send, box_recv,
 ):
     me = lax.axis_index("region")
     row = lax.axis_index("row")
@@ -50,6 +51,14 @@
     for peer in peers:
         pl.semaphore_signal(barrier, inc=1, device_id={"region": peer}, device_id_type=MESH)
 
+    in_copies = []
+    for n, (source, target) in enumerate((
+        (key_hbm, key_ref), (dest_hbm, dest_ref), (local_hbm, local_ref),
+        (limit_hbm, limit_ref), (load_hbm, load_ref),
+    )):
+        copy = pltpu.make_async_copy(source, target, in_sem.at[n])
+        copy.start()
+        in_copies.append(copy)
     own_copies = []
     for c in range(chunks):
         copy = pltpu.make_async_copy(
@@ -59,9 +68,6 @@
         )
         copy.start()
         own_copies.append(copy)
-    ids = (key_ref[...] * regions + dest_ref[...]).astype(F32)
-    id_out[...] = jnp.broadcast_to(ids, id_out.shape)
-
     pl.semaphore_wait(barrier, len(mates) + len(peers))
     full_copies = []
     for c in range(chunks):
@@ -76,6 +82,10 @@
             )
             copy.start()
             full_copies.append((c, j, copy))
+    for copy in in_copies:
+        copy.wait()
+    ids = (key_ref[...] * regions + dest_ref[...]).astype(F32)
+    id_out[...] = jnp.broadcast_to(ids, id_out.shape)
     id_copies = []
     for j, peer in enumerate(peers):
         copy = pltpu.make_async_remote_copy(
@@ -155,17 +165,10 @@
             disp_ref[0] = jnp.clip(value, -limits[...], limits[...])
         if it < ITERS - 1:
             drive[...] = (load_in[...].astype(F32) + prox_in[...] * disp_ref[0]).astype(BF16)
-            gathered[:, :2 * cols] = jnp.zeros((copies, 2 * cols), F32)
-
-            def bulk(i, carry):
-                rows_at = pl.ds(pl.multiple_of(i * step, step), step)
-                prod = wide(full[rows_at, :], drive[...])
-                part[rows_at, :] = prod
-                hi, lo = halves(prod)
-                gathered[:, :2 * cols] += wide(pick[:, rows_at], jnp.concatenate([hi, lo], axis=1))
-                return carry
-
-            lax.fori_loop(0, buses // step, bulk, 0)
+            for at in range(0, buses, half):
+                part[at:at + half, :] = wide(full[at:at + half, :], drive[...])
+            hi, lo = halves(part[...])
+            gathered[:, :2 * cols] = wide(pick[...], jnp.concatenate([hi, lo], axis=1))
         if matches is None:
             id_col = jnp.transpose(jnp.broadcast_to(ids, (copies, copies)))[:, :1]
             for copy in id_copies:
@@ -203,7 +206,7 @@
     return half
 
 
-LINK = F32
+LINK = BF16
 
 
 def per_device(
@@ -224,9 +227,14 @@
             jax.ShapeDtypeStruct((1, buses, cols), F32),
             jax.ShapeDtypeStruct((1, copies, cols), F32),
         ),
-        in_specs=[pl.BlockSpec(memory_space=pl.ANY)] + [vmem] * 5,
+        in_specs=[pl.BlockSpec(memory_space=pltpu.HBM)] * 6,
         out_specs=(vmem, vmem),
         scratch_shapes=[
+            pltpu.VMEM(bus_load.shape, bus_load.dtype),
+            pltpu.VMEM(bus_limit.shape, bus_limit.dtype),
+            pltpu.VMEM(copy_local.shape, copy_local.dtype),
+            pltpu.VMEM(copy_dest.shape, copy_dest.dtype),
+            pltpu.VMEM(copy_key.shape, copy_key.dtype),
             pltpu.VMEM((buses, buses), BF16),
             pltpu.VMEM((buses, cols + copies), BF16),
             pltpu.VMEM((buses, cols), F32),
@@ -241,6 +249,7 @@
             pltpu.VMEM((ITERS, regions - 1, copies, cols), LINK),
             pltpu.VMEM((8, copies), F32),
             pltpu.VMEM((regions - 1, 8, copies), F32),
+            dma((5,)),
             dma((chunks,)),
             dma((rows - 1, chunks)),
             dma((rows - 1, chunks)),
@@ -252,7 +261,7 @@
         compiler_params=pltpu.CompilerParams(
             collective_id=0, has_side_effects=True, vmem_limit_bytes=48 * 1024 * 1024
         ),
-    )(kkt_inverse, bus_load, bus_limit, copy_local, copy_dest, copy_key)
+    )(*[pltpu.with_memory_space_constraint(x, pltpu.HBM) for x in (kkt_inverse, bus_load, bus_limit, copy_local, copy_dest, copy_key)])
 
 
 def solution(mesh):

time: 39.6 us -> 26.5 us (0.67)
  Pallas kernels: 31.8 us -> 24.2 us
  local copies, waits for them, and re-layouts: 6.82 us -> 1.51 us
    pallas_call x1, Pallas kernels: 31.8 us -> 24.2 us  [per_device(): pl.pallas_call(functools.partial(kernel, regions, rows, step, LINK), out_...]
    unnamed x14 -> x2, local copies, waits for them, and re-layouts: 6.82 us -> 1.51 us
where the time goes in v2:
time: 26.5 us; the launch traced here: 26.3 us
  Pallas kernels  24.2 us (91%)
  local copies, waits for them, and re-layouts  1.51 us (6%)
  between operations  0.64 us (2%)
    pallas_call x1, Pallas kernels, per_device(): pl.pallas_call(functools.partial(kernel, regions, rows, step, LINK), out_...  24.2 us
    unnamed x2, local copies, waits for them, and re-layouts  1.51 us

profile of v2, /device:TPU:0, one launch (start us, length us, event | category | flops | bytes accessed | tf_op | source)
XLA Modules:
  0.0 26.3 jit_solution(4306289808611262995)
XLA Ops:
  0.6 24.2 %shard_map.77 = (f32[1,1536,128]{2,1,0:T(8,128)S(1)}, f32[1,128,128]{2,1,0:T(8,128)S(1)}) custom-call(bf16[1,768,1536]{2,1,0:T(8,128)(2,1)} %inv_ref.1, bf16[1,1536,128]{2,1,0:T(8,128)(2,1)} %load_hbm.1, f32[1,1536]{1,0:T(1,128)} %limit_hbm.1, s32[1,128]{1,0:T(1,128)} %local_hbm.1, s32[1,128]{1,0:T(1,128)} %dest_hbm.1, s32[1,128]{1,0:T(1,128)} %key_hbm.1), custom_call_target="tpu_custom_call" | custom-call | tf_op jit(solution)/shard_map/pallas_call | solution.py:224
  24.8 0.9 %copy.10 = f32[1,1536,128]{2,1,0:T(8,128)} copy(f32[1,1536,128]{2,1,0:T(8,128)S(1)} %get-tuple-element.4) | data formatting | bytes 1572864
  25.7 0.6 %copy.11 = f32[1,128,128]{2,1,0:T(8,128)} copy(f32[1,128,128]{2,1,0:T(8,128)S(1)} %get-tuple-element.5) | data formatting | bytes 131072

commit v3 on v2

--- a/solution.py
+++ b/solution.py
@@ -14,6 +14,7 @@
 MESH = pl.DeviceIdType.MESH
 F32 = jnp.float32
 BF16 = jnp.bfloat16
+LINK = BF16
 
 
 def wide(a, b):
@@ -27,13 +28,14 @@
 
 
 def kernel(
-    regions, rows, step, link,
+    regions, rows, step,
     inv_ref, load_hbm, limit_hbm, local_hbm, dest_hbm, key_hbm,
     disp_ref, dual_ref,
     load_ref, limit_ref, local_ref, dest_ref, key_ref,
-    full, first_rhs, part, limits, load_in, prox_in, columns, drive, pick, gathered,
+    full, first_rhs, limits, load_in, prox_in, columns, drive, pick,
+    rows_out, rows_in, rows_at_copies,
     outbox, inbox, id_out, id_in,
-    in_sem, own_sem, full_send, full_recv, id_send, id_recv, box_send, box_recv,
+    in_sem, own_sem, full_send, full_recv, id_send, id_recv, box_send, box_recv, row_send, row_recv,
 ):
     me = lax.axis_index("region")
     row = lax.axis_index("row")
@@ -68,37 +70,10 @@
         )
         copy.start()
         own_copies.append(copy)
-    pl.semaphore_wait(barrier, len(mates) + len(peers))
-    full_copies = []
-    for c in range(chunks):
-        for j, mate in enumerate(mates):
-            copy = pltpu.make_async_remote_copy(
-                src_ref=inv_ref.at[0, pl.ds(c * step, step)],
-                dst_ref=full.at[pl.ds(pl.multiple_of(first_row + c * step, step), step)],
-                send_sem=full_send.at[j, c],
-                recv_sem=full_recv.at[j, c],
-                device_id={"row": mate},
-                device_id_type=MESH,
-            )
-            copy.start()
-            full_copies.append((c, j, copy))
     for copy in in_copies:
         copy.wait()
     ids = (key_ref[...] * regions + dest_ref[...]).astype(F32)
     id_out[...] = jnp.broadcast_to(ids, id_out.shape)
-    id_copies = []
-    for j, peer in enumerate(peers):
-        copy = pltpu.make_async_remote_copy(
-            src_ref=id_out,
-            dst_ref=id_in.at[j],
-            send_sem=id_send.at[j],
-            recv_sem=id_recv.at[j],
-            device_id={"region": peer},
-            device_id_type=MESH,
-        )
-        copy.start()
-        id_copies.append(copy)
-
     local_row = local_ref[...].astype(F32)
     local_col = jnp.transpose(jnp.broadcast_to(local_row, (copies, copies)))[:, :1]
     bus_lane = lax.broadcasted_iota(jnp.int32, (copies, buses), 1).astype(F32)
@@ -120,7 +95,57 @@
     low = (rest - mid.astype(F32)).astype(BF16)
     limit_at = wide(pick[...], top) + wide(pick[...], mid) + wide(pick[...], low)
 
-    gathered[...] = jnp.zeros_like(gathered)
+    for copy in own_copies:
+        copy.wait()
+    own_pick = pick[:, pl.ds(pl.multiple_of(first_row, cols), half)]
+    rows_out[...] = wide(
+        own_pick, full[pl.ds(pl.multiple_of(first_row, step), half), :]
+    ).astype(BF16)
+    pl.semaphore_wait(barrier, len(mates) + len(peers))
+    row_copies = []
+    for j, mate in enumerate(mates):
+        copy = pltpu.make_async_remote_copy(
+            src_ref=rows_out,
+            dst_ref=rows_in.at[j],
+            send_sem=row_send.at[j],
+            recv_sem=row_recv.at[j],
+            device_id={"row": mate},
+            device_id_type=MESH,
+        )
+        copy.start()
+        row_copies.append(copy)
+    id_copies = []
+    for j, peer in enumerate(peers):
+        copy = pltpu.make_async_remote_copy(
+            src_ref=id_out,
+            dst_ref=id_in.at[j],
+            send_sem=id_send.at[j],
+            recv_sem=id_recv.at[j],
+            device_id={"region": peer},
+            device_id_type=MESH,
+        )
+        copy.start()
+        id_copies.append(copy)
+
+    full_copies = []
+    for c in range(chunks):
+        for j, mate in enumerate(mates):
+            copy = pltpu.make_async_remote_copy(
+                src_ref=inv_ref.at[0, pl.ds(c * step, step)],
+                dst_ref=full.at[pl.ds(pl.multiple_of(first_row + c * step, step), step)],
+                send_sem=full_send.at[j, c],
+                recv_sem=full_recv.at[j, c],
+                device_id={"row": mate},
+                device_id_type=MESH,
+            )
+            copy.start()
+            full_copies.append((c, j, copy))
+    at_rows = rows_out[...]
+    for j, copy in enumerate(row_copies):
+        copy.wait()
+        at_rows = at_rows + rows_in[j]
+    rows_at_copies[...] = at_rows
+    at_copies = jnp.clip(wide(rows_at_copies[...], load_ref[0]), -limit_at, limit_at)
 
     def first_chunk(at):
         at = pl.multiple_of(at, step)
@@ -131,23 +156,13 @@
         bound = limits[rows_at, :]
         value = jnp.clip(prod[:, :cols], -bound, bound)
         disp_ref[0, rows_at, :] = value
-        hi, lo = halves(value)
-        gathered[...] += wide(pick[:, rows_at], jnp.concatenate([hi, lo, picked], axis=1))
-
-    for c in range(chunks):
-        own_copies[c].wait()
-        first_chunk(first_row + c * step)
-    for c, j, copy in full_copies:
-        copy.wait()
-        first_chunk(lax.rem(row + rows - j - 1, rows) * half + c * step)
-    at_copies = gathered[:, :cols] + gathered[:, cols:2 * cols]
-    columns_at = gathered[:, 2 * cols:].astype(BF16)
+
     duals = jnp.zeros((copies, cols), F32)
 
     matches = None
     for it in range(ITERS):
         shared = at_copies + duals
-        outbox[it] = shared.astype(link)
+        outbox[it] = shared.astype(LINK)
         box_copies = []
         for j, peer in enumerate(peers):
             copy = pltpu.make_async_remote_copy(
@@ -160,41 +175,45 @@
             )
             copy.start()
             box_copies.append(copy)
-        if it > 0:
-            value = part[...] + wide(columns[...], drive_at)
-            disp_ref[0] = jnp.clip(value, -limits[...], limits[...])
+        if it == 0:
+            for c in range(chunks):
+                first_chunk(first_row + c * step)
+            for c, j, copy in full_copies:
+                copy.wait()
+                first_chunk(lax.rem(row + rows - j - 1, rows) * half + c * step)
+            columns_at = wide(rows_at_copies[...], first_rhs[:, cols:]).astype(BF16)
+        else:
+            for at in range(0, buses, half):
+                value = wide(full[at:at + half, :], drive[...])
+                value = value + wide(columns[at:at + half, :], drive_at)
+                bound = limits[at:at + half, :]
+                disp_ref[0, at:at + half, :] = jnp.clip(value, -bound, bound)
         if it < ITERS - 1:
             drive[...] = (load_in[...].astype(F32) + prox_in[...] * disp_ref[0]).astype(BF16)
-            for at in range(0, buses, half):
-                part[at:at + half, :] = wide(full[at:at + half, :], drive[...])
-            hi, lo = halves(part[...])
-            gathered[:, :2 * cols] = wide(pick[...], jnp.concatenate([hi, lo], axis=1))
+            inner_at = wide(rows_at_copies[...], drive[...])
         if matches is None:
             id_col = jnp.transpose(jnp.broadcast_to(ids, (copies, copies)))[:, :1]
             for copy in id_copies:
                 copy.wait()
-            matches = [jnp.where(id_col == ids, 1.0, 0.0).astype(BF16)]
-            for j in range(regions - 1):
-                matches.append(jnp.where(id_col == id_in[j, :1, :], 1.0, 0.0).astype(BF16))
-            tally = functools.reduce(
-                lambda a, b: a + b, [wide(m, jnp.ones((copies, cols), BF16)) for m in matches]
-            )
+            own_match = jnp.where(id_col == ids, 1.0, 0.0).astype(BF16)
+            matches = jnp.concatenate([
+                jnp.where(id_col == id_in[j, :1, :], 1.0, 0.0).astype(BF16)
+                for j in range(regions - 1)
+            ], axis=1)
+            tally = wide(own_match, jnp.ones((copies, cols), BF16))
+            tally += wide(matches, jnp.ones((matches.shape[1], cols), BF16))
             tally = jnp.maximum(tally, 1.0)
         hi, lo = halves(shared)
-        total = wide(matches[0], hi) + wide(matches[0], lo)
-        for j, copy in enumerate(box_copies):
+        total = wide(own_match, hi) + wide(own_match, lo)
+        for copy in box_copies:
             copy.wait()
-            if link == F32:
-                hi, lo = halves(inbox[it, j])
-                total += wide(matches[j + 1], hi) + wide(matches[j + 1], lo)
-            else:
-                total += wide(matches[j + 1], inbox[it, j])
+        total += wide(matches, inbox[it].reshape(matches.shape[1], cols))
         consensus = total / tally
         duals = duals + at_copies - consensus
         if it < ITERS - 1:
             boundary = consensus - duals
             drive_at = (load_at + PROXIMAL * at_copies + PENALTY * boundary).astype(BF16)
-            solved_at = gathered[:, :cols] + gathered[:, cols:2 * cols] + wide(columns_at, drive_at)
+            solved_at = inner_at + wide(columns_at, drive_at)
             at_copies = jnp.clip(solved_at, -limit_at, limit_at)
     dual_ref[0] = duals
 
@@ -204,9 +223,6 @@
         if half % step == 0:
             return step
     return half
-
-
-LINK = BF16
 
 
 def per_device(
@@ -222,7 +238,7 @@
     dma = pltpu.SemaphoreType.DMA
     vmem = pl.BlockSpec(memory_space=pltpu.VMEM)
     return pl.pallas_call(
-        functools.partial(kernel, regions, rows, step, LINK),
+        functools.partial(kernel, regions, rows, step),
         out_shape=(
             jax.ShapeDtypeStruct((1, buses, cols), F32),
             jax.ShapeDtypeStruct((1, copies, cols), F32),
@@ -238,13 +254,14 @@
             pltpu.VMEM((buses, buses), BF16),
             pltpu.VMEM((buses, cols + copies), BF16),
             pltpu.VMEM((buses, cols), F32),
-            pltpu.VMEM((buses, cols), F32),
             pltpu.VMEM((buses, cols), BF16),
             pltpu.VMEM((buses, cols), F32),
             pltpu.VMEM((buses, copies), BF16),
             pltpu.VMEM((buses, cols), BF16),
             pltpu.VMEM((copies, buses), BF16),
-            pltpu.VMEM((copies, 2 * cols + copies), F32),
+            pltpu.VMEM((copies, buses), BF16),
+            pltpu.VMEM((rows - 1, copies, buses), BF16),
+            pltpu.VMEM((copies, buses), BF16),
             pltpu.VMEM((ITERS, copies, cols), LINK),
             pltpu.VMEM((ITERS, regions - 1, copies, cols), LINK),
             pltpu.VMEM((8, copies), F32),
@@ -257,6 +274,8 @@
             dma((regions - 1,)),
             dma((ITERS, regions - 1)),
             dma((ITERS, regions - 1)),
+            dma((rows - 1,)),
+            dma((rows - 1,)),
         ],
         compiler_params=pltpu.CompilerParams(
             collective_id=0, has_side_effects=True, vmem_limit_bytes=48 * 1024 * 1024

time: 26.5 us -> 24.8 us (0.936)
  Pallas kernels: 24.2 us -> 22.5 us
    pallas_call x1, Pallas kernels: 24.2 us -> 22.5 us  [per_device(): pl.pallas_call(functools.partial(kernel, regions, rows, step), out_shape=...]
where the time goes in v3:
time: 24.8 us; the launch traced here: 24.7 us
  Pallas kernels  22.5 us (91%)
  local copies, waits for them, and re-layouts  1.51 us (6%)
  between operations  0.64 us (3%)
    pallas_call x1, Pallas kernels, per_device(): pl.pallas_call(functools.partial(kernel, regions, rows, step), out_shape=...  22.5 us
    unnamed x2, local copies, waits for them, and re-layouts  1.51 us

profile of v3, /device:TPU:0, one launch (start us, length us, event | category | flops | bytes accessed | tf_op | source)
XLA Modules:
  0.0 24.7 jit_solution(10949317512926857106)
XLA Ops:
  0.6 22.5 %shard_map.77 = (f32[1,1536,128]{2,1,0:T(8,128)S(1)}, f32[1,128,128]{2,1,0:T(8,128)S(1)}) custom-call(bf16[1,768,1536]{2,1,0:T(8,128)(2,1)} %inv_ref.1, bf16[1,1536,128]{2,1,0:T(8,128)(2,1)} %load_hbm.1, f32[1,1536]{1,0:T(1,128)} %limit_hbm.1, s32[1,128]{1,0:T(1,128)} %local_hbm.1, s32[1,128]{1,0:T(1,128)} %dest_hbm.1, s32[1,128]{1,0:T(1,128)} %key_hbm.1), custom_call_target="tpu_custom_call" | custom-call | tf_op jit(solution)/shard_map/pallas_call | solution.py:240
  23.2 0.9 %copy.10 = f32[1,1536,128]{2,1,0:T(8,128)} copy(f32[1,1536,128]{2,1,0:T(8,128)S(1)} %get-tuple-element.4) | data formatting | bytes 1572864
  24.1 0.6 %copy.11 = f32[1,128,128]{2,1,0:T(8,128)} copy(f32[1,128,128]{2,1,0:T(8,128)S(1)} %get-tuple-element.5) | data formatting | bytes 131072
